TPU v7x, 256 devices: a whole 4x4x8 slice. The times are simulated.
256 devices in a mesh: seq: 64 (over z, y_hi, x), head: 4 (over y_lo, core).
Axes of the slice: x: 4, y: 4 (y_hi: 2, y_lo: 2; y = y_hi * 2 + y_lo), z: 8, core: 2. Of those that a mesh axis runs over, the one named last changes fastest.
Arguments:
- queries: bfloat16 [32768, 4096], P('seq', 'head'), may hold values from -4.5 to 4.5
- key_heads: bfloat16 [32768, 1024], P('seq', 'head'), may hold values from -4.5 to 4.5
- value_head_rows: bfloat16 [32768, 1024], P('seq', 'head'), may hold values from -6 to 6
- out_grad: bfloat16 [32768, 4096], P('seq', 'head'), may hold values from -6 to 6
- doc_ids: int32 [32768], P('seq'), may hold values from 0 to 63, never falling along the last dimension, each value on 1 to 2048 neighbouring positions
Outputs:
- query_grad: bfloat16 [32768, 4096], P(('seq', 'head'))
- key_grad: bfloat16 [32768, 1024], P('seq', 'head')
- value_grad: bfloat16 [32768, 1024], P('seq', 'head')
Inputs may be any that keep to these rules, and one draw needn't show every extreme that they name: `doc_ids`: never falling along the sequence; each document is 1 to 2048 tokens long and one is exactly 2048.
All inputs are finite; a program needn't handle non-finite values.
Results may differ from a plain program's by a relative error of at most 0.0072.
Values may be sent and summed in bfloat16 or wider, within the bound.
A program may use at most 128 MiB of HBM per device.

v0:
```python
import math

import jax
import jax.numpy as jnp
from jax import lax
from jax.sharding import PartitionSpec as P

HEAD_SIZE = 128


masked_fill = -1e30


def shifted(value, axis, by):
    count = lax.axis_size(axis)
    pairs = [(i, i + by) for i in range(count) if 0 <= i + by < count]
    return lax.ppermute(value, axis, pairs)


def split_rows(matrix, groups):
    return matrix.reshape(matrix.shape[0], groups, -1, HEAD_SIZE)


def split_keys(matrix, groups):
    return matrix.reshape(matrix.shape[0], groups, HEAD_SIZE)


def score_block(query_pieces, key_pieces, keep_mask, score_scale):
    scores = (
        jnp.einsum("rhgd,khd->hgrk", query_pieces, key_pieces, preferred_element_type=jnp.float32)
        * score_scale
    )
    return jnp.where(keep_mask, scores, masked_fill)


def partial_stats(scores, keep_mask):
    row_top = jnp.max(scores, axis=-1)
    row_sum = jnp.sum(jnp.where(keep_mask, jnp.exp(scores - row_top[..., None]), 0.0), axis=-1)
    return (row_top, row_sum)


def joined_stats(top_own, sum_own, top_other, sum_other):
    joint_top = jnp.maximum(top_own, top_other)
    return joint_top + jnp.log(
        sum_own * jnp.exp(top_own - joint_top) + sum_other * jnp.exp(top_other - joint_top)
    )


def probabilities(scores, keep_mask, log_total):
    return jnp.where(keep_mask, jnp.exp(scores - log_total[..., None]), 0.0)


def value_terms(gradient_pieces, value_pieces):
    return jnp.einsum(
        "rhgd,khd->hgrk", gradient_pieces, value_pieces, preferred_element_type=jnp.float32
    )


def block_gradients(
    probs_full, grad_probs, delta_rows, query_pieces, gradient_pieces, key_pieces, score_scale
):
    grad_scores = (probs_full * (grad_probs - delta_rows[..., None])).astype(jnp.bfloat16)
    probs_round = probs_full.astype(jnp.bfloat16)
    row_number = query_pieces.shape[0]
    key_number = key_pieces.shape[0]
    query_portion = (
        jnp.einsum("hgrk,khd->rhgd", grad_scores, key_pieces, preferred_element_type=jnp.float32)
        * score_scale
    )
    key_portion = (
        jnp.einsum("hgrk,rhgd->khd", grad_scores, query_pieces, preferred_element_type=jnp.float32)
        * score_scale
    )
    value_portion = jnp.einsum(
        "hgrk,rhgd->khd", probs_round, gradient_pieces, preferred_element_type=jnp.float32
    )
    return (
        query_portion.reshape(row_number, -1),
        key_portion.reshape(key_number, -1),
        value_portion.reshape(key_number, -1),
    )


def local(queries, key_heads, value_head_rows, out_grad, doc_ids):
    row_number = queries.shape[0]
    kv_groups = key_heads.shape[1] // HEAD_SIZE
    score_scale = 1.0 / math.sqrt(HEAD_SIZE)
    seq_index = lax.axis_index("seq")
    query_pieces = split_rows(queries, kv_groups)
    gradient_pieces = split_rows(out_grad, kv_groups)
    key_pieces = split_keys(key_heads, kv_groups)
    value_pieces = split_keys(value_head_rows, kv_groups)
    positions = jnp.arange(row_number)
    lower_tri = positions[None, :] <= positions[:, None]
    upper_tri = positions[None, :] > positions[:, None]
    diag_mask = lower_tri & (doc_ids[:, None] == doc_ids[None, :])
    scores_own = score_block(query_pieces, key_pieces, diag_mask, score_scale)
    top_own, sum_own = partial_stats(scores_own, diag_mask)
    grad_own = value_terms(gradient_pieces, value_pieces)
    owner_valid = seq_index > 0
    key_prev, value_prev, doc_prev = shifted((key_heads, value_head_rows, doc_ids), "seq", 1)
    key_prev_split = split_keys(key_prev, kv_groups)
    value_prev_split = split_keys(value_prev, kv_groups)
    cross_mask = upper_tri & (doc_ids[:, None] == doc_prev[None, :]) & owner_valid
    scores_cross = score_block(query_pieces, key_prev_split, cross_mask, score_scale)
    top_cross, sum_cross = partial_stats(scores_cross, cross_mask)
    log_total = joined_stats(top_own, sum_own, top_cross, sum_cross)
    probs_own = probabilities(scores_own, diag_mask, log_total)
    probs_cross = probabilities(scores_cross, cross_mask, log_total)
    grad_cross = value_terms(gradient_pieces, value_prev_split)
    delta_rows = jnp.sum(probs_own * grad_own, axis=-1) + jnp.sum(probs_cross * grad_cross, axis=-1)
    dq_own, dk_own, dv_own = block_gradients(
        probs_own, grad_own, delta_rows, query_pieces, gradient_pieces, key_pieces, score_scale
    )
    dq_cross, dk_cross, dv_cross = block_gradients(
        probs_cross,
        grad_cross,
        delta_rows,
        query_pieces,
        gradient_pieces,
        key_prev_split,
        score_scale,
    )
    dk_next, dv_next = shifted((dk_cross, dv_cross), "seq", -1)
    query_total = dq_own + dq_cross
    key_total = dk_own + dk_next
    value_total = dv_own + dv_next
    query_grad = lax.all_to_all(
        query_total.astype(jnp.bfloat16), "head", split_axis=0, concat_axis=1, tiled=True
    )
    return (query_grad, key_total.astype(jnp.bfloat16), value_total.astype(jnp.bfloat16))


def solution(mesh):
    placed = (P("seq", "head"), P("seq", "head"), P("seq", "head"), P("seq", "head"), P("seq"))
    return jax.shard_map(
        local,
        mesh=mesh,
        in_specs=placed,
        out_specs=(P(("seq", "head"), None), P("seq", "head"), P("seq", "head")),
        check_vma=False,
    )
```

profile of v0, /device:TPU:102, one launch (start us, length us, event | category | flops | bytes accessed | tf_op | source)
XLA Modules:
  0.0 115.8 jit_solution(16188124262718538952)
XLA Ops:
  0.6 0.0 copy-start.7
  0.6 0.0 copy-start.5
  0.7 5.1 %collective-permute-start = (s32[512]{0:T(512)}, s32[512]{0:T(512)S(1)}, u32[]{:S(2)}, u32[]{:S(2)}) collective-permute-start(s32[512]{0:T(512)} %param.9), channel_id=1, source_target_pairs={{0,4},{4,8},{8,12},{12,16},{16,20},{20,24},{24,28},{28,32},{32,36}... | collective-permute-start | bytes 6152 | tf_op jit(solution)/shard_map/ppermute | solution.py:17
  5.8 1.1 copy.63
  6.9 3.4 %collective-permute-start.2 = (bf16[512,256]{0,1:T(8,128)(2,1)S(1)}, bf16[512,256]{0,1:T(8,128)(2,1)}, u32[]{:S(2)}, u32[]{:S(2)}) collective-permute-start(bf16[512,256]{0,1:T(8,128)(2,1)S(1)} %copy.63), channel_id=1, source_target_pairs={{0,4},{4,8},{8,12},{12,16},{16,20},{20,24},{24,28},{28,32},{32,36}... | collective-permute-start | bytes 786440 | tf_op jit(solution)/shard_map/ppermute | solution.py:17
  10.3 1.8 %copy.58 = bf16[512,256]{0,1:T(8,128)(2,1)} copy(bf16[512,256]{1,0:T(8,128)(2,1)} %param.6) | data formatting | bytes 524288 | tf_op args[1]
  12.1 3.4 %collective-permute-start.1 = (bf16[512,256]{0,1:T(8,128)(2,1)}, bf16[512,256]{0,1:T(8,128)(2,1)S(1)}, u32[]{:S(2)}, u32[]{:S(2)}) collective-permute-start(bf16[512,256]{0,1:T(8,128)(2,1)} %copy.58), channel_id=1, source_target_pairs={{0,4},{4,8},{8,12},{12,16},{16,20},{20,24},{24,28},{28,32},{32,36}... | collective-permute-start | bytes 786440 | tf_op jit(solution)/shard_map/ppermute | solution.py:17
  15.5 1.0 reshape.76
  16.5 1.5 %copy.114 = bf16[512,1024]{0,1:T(8,128)(2,1)S(1)} copy(bf16[512,1024]{1,0:T(8,128)(2,1)} %param.8) | data formatting | bytes 2097152 | tf_op jit(solution)/shard_map/reshape | solution.py:21
  18.0 4.5 %fusion.18 = f32[2,512,512,4]{2,1,3,0:T(8,128)} fusion(bf16[512,2,4,128]{0,3,2,1:T(8,128)(2,1)S(1)} %bitcast.120, bf16[512,2,128,1]{2,1,0,3:T(2,128)(2,1)S(1)} %bitcast.130), kind=kOutput, calls=%fused_computation.35 | convolution fusion | flops 536870912 | bytes 9699328 | tf_op jit(solution)/shard_map/rhgd,khd->hgrk/dot_general | solution.py:54
  22.5 0.0 copy-done.5
  22.5 0.1 reshape.73
  22.6 1.5 %copy.113 = bf16[512,1024]{0,1:T(8,128)(2,1)S(1)} copy(bf16[512,1024]{1,0:T(8,128)(2,1)} %param.5) | data formatting | bytes 2097152 | tf_op jit(solution)/shard_map/reshape | solution.py:21
  24.1 0.0 collective-permute-done
  24.1 0.0 copy-done.7
  24.1 0.4 fusion.15
  24.5 1.6 %fusion.6 = (f32[2,4,512]{2,1,0:T(4,128)S(1)}, f32[2,512,512,4]{2,1,3,0:T(8,128)S(1)}) fusion(pred[512,512]{0,1:T(8,128)(4,1)S(1)} %get-tuple-element.10, bf16[512,2,4,128]{0,3,2,1:T(8,128)(2,1)S(1)} %bitcast.116, bf16[512,2,128,1]{2,1,0,3:T(2,128)(2,1)S(1)} %bitcast.126), kind=kOutput, calls=%fused_computation.16 | convolution fusion | flops 543158272 | bytes 9977856 | tf_op jit(solution)/shard_map/rhgd,khd->hgrk/dot_general | solution.py:30
  26.1 0.0 copy-start
  26.1 2.0 %select_reduce_fusion.1 = f32[2,4,512]{2,1,0:T(4,128)S(1)} fusion(f32[2,512,512,4]{2,1,3,0:T(8,128)S(1)} %get-tuple-element.15, f32[2,4,512]{2,1,0:T(4,128)S(1)} %get-tuple-element.14, pred[512,512]{0,1:T(8,128)(4,1)S(1)} %get-tuple-element.10), kind=kLoop, calls=%fused_computation.15 | loop fusion | flops 10481664 | bytes 8683520 | tf_op jit(solution)/shard_map/reduce_sum | solution.py:38
  28.1 0.0 collective-permute-done.1
  28.1 1.6 %fusion.7 = (f32[2,4,512]{2,1,0:T(4,128)S(1)}, f32[2,512,512,4]{2,1,3,0:T(8,128)S(1)}) fusion(pred[512,512]{0,1:T(8,128)(4,1)S(1)} %get-tuple-element.11, bf16[512,2,128,1]{0,2,3,1:T(8,128)(2,1)S(1)} %bitcast.131, bf16[512,2,4,128]{0,3,2,1:T(8,128)(2,1)S(1)} %bitcast.117), kind=kOutput, calls=%fused_computation.17 | convolution fusion | flops 543158272 | bytes 9977856 | tf_op jit(solution)/shard_map/rhgd,khd->hgrk/dot_general | solution.py:30
  29.7 0.0 copy-start.1
  29.7 2.0 %select_reduce_fusion = f32[2,4,512]{2,1,0:T(4,128)S(1)} fusion(f32[2,512,512,4]{2,1,3,0:T(8,128)S(1)} %get-tuple-element.13, f32[2,4,512]{2,1,0:T(4,128)S(1)} %get-tuple-element.12, pred[512,512]{0,1:T(8,128)(4,1)S(1)} %get-tuple-element.11), kind=kLoop, calls=%fused_computation.14 | loop fusion | flops 10481664 | bytes 8683520 | tf_op jit(solution)/shard_map/reduce_sum | solution.py:38
  31.8 3.3 %fusion.8 = f32[2,512,128,1]{1,2,3,0:T(8,128)} fusion(bf16[512,2,4,128]{0,3,2,1:T(8,128)(2,1)S(1)} %bitcast.121, f32[2,512,512,4]{2,1,3,0:T(8,128)S(1)} %get-tuple-element.13, f32[2,4,512]{2,1,0:T(4,128)S(1)} %bitcast.137, pred[512,512]{0,1:T(8,128)(4,1)S(1)} %get-tuple-element.11), kind=kOutput, calls=%fused_computation.18 | convolution fusion | flops 547356672 | bytes 10240000 | tf_op jit(solution)/shard_map/hgrk,rhgd->khd/dot_general | solution.py:74
  35.1 0.0 copy-done
  35.1 0.0 copy-done.1
  35.1 3.2 %fusion.10 = f32[2,512,128,1]{1,2,3,0:T(8,128)} fusion(bf16[512,2,4,128]{0,3,2,1:T(8,128)(2,1)S(1)} %bitcast.122, f32[2,512,512,4]{2,1,3,0:T(8,128)S(1)} %get-tuple-element.15, f32[2,4,512]{2,1,0:T(4,128)S(1)} %bitcast.138, pred[512,512]{0,1:T(8,128)(4,1)S(1)} %get-tuple-element.10), kind=kOutput, calls=%fused_computation.20 | convolution fusion | flops 547356672 | bytes 10240000 | tf_op jit(solution)/shard_map/hgrk,rhgd->khd/dot_general | solution.py:74
  38.3 2.0 %copy.82 = f32[512,256]{1,0:T(8,128)} copy(f32[512,256]{0,1:T(8,128)} %bitcast.134) | data formatting | bytes 1048576 | tf_op jit(solution)/shard_map/reshape | solution.py:80
  40.4 2.6 %collective-permute-start.4 = (f32[512,256]{1,0:T(8,128)}, f32[512,256]{1,0:T(8,128)}, u32[]{:S(2)}, u32[]{:S(2)}) collective-permute-start(f32[512,256]{1,0:T(8,128)} %copy.82), channel_id=1, source_target_pairs={{4,0},{8,4},{12,8},{16,12},{20,16},{24,20},{28,24},{32,28},{36,32}... | collective-permute-start | bytes 1572872 | tf_op jit(solution)/shard_map/ppermute | solution.py:17
  43.0 0.0 collective-permute-done.2
  43.0 13.1 %fusion = (f32[2,4,512]{2,1,0:T(4,128)S(1)}, f32[2,4,512]{2,1,0:T(4,128)S(1)}, f32[2,512,512,4]{2,1,3,0:T(8,128)}) fusion(f32[2,4,512]{2,1,0:T(4,128)S(1)} %bitcast.139, f32[2,512,512,4]{2,1,3,0:T(8,128)} %copy-done.1, pred[512,512]{0,1:T(8,128)(4,1)S(1)} %get-tuple-element.11, f32[2,512,512,4]{2,1,3,0:T(8,128)} %fusion.18, f32[2,512,512,4]{2,1,3,0:T(8,128)} %copy-done, ...), kind=kOutput, calls=%fused_computation.2 | convolution fusion | flops 562028544 | bytes 35438592 | tf_op jit(solution)/shard_map/rhgd,khd->hgrk/dot_general | solution.py:54
  56.1 15.2 %fusion.2 = (bf16[2,4,512,512]{2,3,1,0:T(8,128)(2,1)}, bf16[2,4,512,512]{2,3,1,0:T(8,128)(2,1)S(1)}) fusion(f32[2,512,512,4]{2,1,3,0:T(8,128)} %get-tuple-element.16, f32[2,4,512]{2,1,0:T(4,128)S(1)} %add.35, f32[2,4,512]{2,1,0:T(4,128)S(1)} %bitcast.140, f32[2,512,512,4]{2,1,3,0:T(8,128)} %copy-done.1, pred[512,512]{0,1:T(8,128)(4,1)S(1)} %get-tuple-element.11, ...), kind=kLoop, calls=%fused_computation.4 | loop fusion | flops 29360128 | bytes 42500096 | tf_op jit(solution)/shard_map/convert_element_type | solution.py:62
  71.4 0.0 copy-start.2
  71.4 0.0 copy-start.3
  71.4 0.0 copy-start.6
  71.4 1.8 %fusion.20 = f32[2,4,512,128]{3,2,1,0:T(8,128)S(1)} fusion(bf16[2,4,512,512]{2,3,1,0:T(8,128)(2,1)S(1)} %get-tuple-element.9, bf16[512,2,128,1]{2,1,0,3:T(2,128)(2,1)S(1)} %bitcast.127), kind=kOutput, calls=%fused_computation.37 | convolution fusion | flops 536870912 | bytes 6553600 | tf_op jit(solution)/shard_map/hgrk,khd->rhgd/dot_general | solution.py:67
  73.1 1.9 %copy-done.3 = bf16[2,4,512,512]{2,3,1,0:T(8,128)(2,1)S(1)} copy-done((bf16[2,4,512,512]{2,3,1,0:T(8,128)(2,1)S(1)}, bf16[2,4,512,512]{2,3,1,0:T(8,128)(2,1)}, u32[]{:S(2)}) %copy-start.3) | copy-done | bytes 4194328
  75.1 1.8 %fusion.12 = bf16[512,2,4,128]{3,0,2,1:T(8,128)(2,1)S(1)} fusion(f32[2,4,512,128]{3,2,1,0:T(8,128)S(1)} %fusion.20, bf16[2,4,512,512]{2,3,1,0:T(8,128)(2,1)S(1)} %copy-done.3, bf16[512,2,128,1]{0,2,3,1:T(8,128)(2,1)S(1)} %bitcast.132), kind=kOutput, calls=%fused_computation.23 | convolution fusion | flops 538443776 | bytes 7602176 | tf_op jit(solution)/shard_map/hgrk,khd->rhgd/dot_general | solution.py:67
  76.9 2.3 %fusion.14 = f32[2,512,128]{1,2,0:T(8,128)} fusion(bf16[2,4,512,512]{2,3,1,0:T(8,128)(2,1)S(1)} %copy-done.3, bf16[512,2,4,128]{0,3,2,1:T(8,128)(2,1)S(1)} %bitcast.118), kind=kOutput, calls=%fused_computation.27 | convolution fusion | flops 537001984 | bytes 5767168 | tf_op jit(solution)/shard_map/hgrk,rhgd->khd/dot_general | solution.py:71
  79.2 0.0 copy-done.2
  79.2 0.0 copy-done.6
  79.2 1.0 copy.83
  80.2 0.8 copy.70
  81.0 0.0 copy-start.4
  81.0 1.5 %convert_element_type.32 = bf16[4,128,1024]{2,1,0:T(8,128)(2,1)} reshape(bf16[512,2,4,128]{3,2,1,0:T(4,128)(2,1)S(1)} %copy.70) | data formatting | bytes 2097152 | tf_op jit(solution)/shard_map/convert_element_type | solution.py:129
  82.6 2.0 %copy.76 = f32[512,256]{1,0:T(8,128)} copy(f32[512,256]{0,1:T(8,128)} %bitcast.128) | data formatting | bytes 1048576 | tf_op jit(solution)/shard_map/reshape | solution.py:79
  84.6 3.5 %all-to-all-start = ((bf16[4,128,1024]{2,1,0:T(8,128)(2,1)}), bf16[4,128,1024]{2,1,0:T(8,128)(2,1)S(1)}, u32[]{:S(2)}, u32[]{:S(2)}) async-start(bf16[4,128,1024]{2,1,0:T(8,128)(2,1)} %convert_element_type.32), calls=%async_computation | async-start | bytes 2097152 | tf_op jit(solution)/shard_map/all_to_all | solution.py:128
  88.1 2.4 %collective-permute-start.3 = (f32[512,256]{1,0:T(8,128)}, f32[512,256]{1,0:T(8,128)}, u32[]{:S(2)}, u32[]{:S(2)}) collective-permute-start(f32[512,256]{1,0:T(8,128)} %copy.76), channel_id=1, source_target_pairs={{4,0},{8,4},{12,8},{16,12},{20,16},{24,20},{28,24},{32,28},{36,32}... | collective-permute-start | bytes 1572872 | tf_op jit(solution)/shard_map/ppermute | solution.py:17
  90.6 3.6 %fusion.13 = f32[2,512,128]{1,2,0:T(8,128)S(1)} fusion(bf16[2,4,512,512]{2,3,1,0:T(8,128)(2,1)} %copy-done.2, bf16[512,2,4,128]{0,3,2,1:T(8,128)(2,1)S(1)} %bitcast.119), kind=kOutput, calls=%fused_computation.26 | convolution fusion | flops 537001984 | bytes 5767168 | tf_op jit(solution)/shard_map/hgrk,rhgd->khd/dot_general | solution.py:71
  94.2 0.2 copy.77
  94.4 0.0 collective-permute-done.4
  94.4 0.0 copy-done.4
  94.5 1.8 %add_convert_fusion = bf16[512,256]{1,0:T(8,128)(2,1)} fusion(f32[512,256]{1,0:T(8,128)S(1)} %copy-done.4, f32[512,256]{1,0:T(8,128)} %collective-permute-done.4), kind=kLoop, calls=%fused_computation.33 | loop fusion | flops 262144 | bytes 1310720 | tf_op jit(solution)/shard_map/convert_element_type | solution.py:131
  96.3 12.1 %collective-permute-done.3 = f32[512,256]{1,0:T(8,128)} collective-permute-done((f32[512,256]{1,0:T(8,128)}, f32[512,256]{1,0:T(8,128)}, u32[]{:S(2)}, u32[]{:S(2)}) %collective-permute-start.3) | collective-permute-done | bytes 524320 | tf_op jit(solution)/shard_map/ppermute | solution.py:17
  108.3 1.8 %add_convert_fusion.1 = bf16[512,256]{1,0:T(8,128)(2,1)} fusion(f32[512,256]{1,0:T(8,128)S(1)} %copy.77, f32[512,256]{1,0:T(8,128)} %collective-permute-done.3), kind=kLoop, calls=%fused_computation.34 | loop fusion | flops 262144 | bytes 1310720 | tf_op jit(solution)/shard_map/convert_element_type | solution.py:131
  110.1 3.7 %all-to-all-done = bf16[4,128,1024]{2,1,0:T(8,128)(2,1)S(1)} async-done(((bf16[4,128,1024]{2,1,0:T(8,128)(2,1)}), bf16[4,128,1024]{2,1,0:T(8,128)(2,1)S(1)}, u32[]{:S(2)}, u32[]{:S(2)}) %all-to-all-start) | async-done | bytes 1048608 | tf_op jit(solution)/shard_map/all_to_all | solution.py:128
  113.8 0.7 copy.71
  114.5 1.3 %copy.84 = bf16[128,4096]{1,0:T(8,128)(2,1)} copy(bf16[128,4096]{0,1:T(8,128)(2,1)S(1)} %bitcast.125) | data formatting | bytes 2097152
  (2 shorter events, 0.0 us)
Async XLA Ops:
  0.6 23.5 %copy-start.7 = (s32[512]{0:T(512)S(1)}, s32[512]{0:T(512)}, u32[]{:S(2)}) copy-start(s32[512]{0:T(512)} %param.9) | copy-start | bytes 6148
  0.6 21.9 %copy-start.5 = (bf16[512,256]{1,0:T(8,128)(2,1)S(1)}, bf16[512,256]{1,0:T(8,128)(2,1)}, u32[]{:S(2)}) copy-start(bf16[512,256]{1,0:T(8,128)(2,1)} %param.6) | copy-start | bytes 786436
  0.7 23.4 %collective-permute-start = (s32[512]{0:T(512)}, s32[512]{0:T(512)S(1)}, u32[]{:S(2)}, u32[]{:S(2)}) collective-permute-start(s32[512]{0:T(512)} %param.9), channel_id=1, source_target_pairs={{0,4},{4,8},{8,12},{12,16},{16,20},{20,24},{24,28},{28,32},{32,36}... | collective-permute-start | bytes 6152 | tf_op jit(solution)/shard_map/ppermute | solution.py:17
  6.9 36.1 %collective-permute-start.2 = (bf16[512,256]{0,1:T(8,128)(2,1)S(1)}, bf16[512,256]{0,1:T(8,128)(2,1)}, u32[]{:S(2)}, u32[]{:S(2)}) collective-permute-start(bf16[512,256]{0,1:T(8,128)(2,1)S(1)} %copy.63), channel_id=1, source_target_pairs={{0,4},{4,8},{8,12},{12,16},{16,20},{20,24},{24,28},{28,32},{32,36}... | collective-permute-start | bytes 786440 | tf_op jit(solution)/shard_map/ppermute | solution.py:17
  12.1 16.0 %collective-permute-start.1 = (bf16[512,256]{0,1:T(8,128)(2,1)}, bf16[512,256]{0,1:T(8,128)(2,1)S(1)}, u32[]{:S(2)}, u32[]{:S(2)}) collective-permute-start(bf16[512,256]{0,1:T(8,128)(2,1)} %copy.58), channel_id=1, source_target_pairs={{0,4},{4,8},{8,12},{12,16},{16,20},{20,24},{24,28},{28,32},{32,36}... | collective-permute-start | bytes 786440 | tf_op jit(solution)/shard_map/ppermute | solution.py:17
  26.1 9.1 %copy-start = (f32[2,512,512,4]{2,1,3,0:T(8,128)}, f32[2,512,512,4]{2,1,3,0:T(8,128)S(1)}, u32[]{:S(2)}) copy-start(f32[2,512,512,4]{2,1,3,0:T(8,128)S(1)} %get-tuple-element.15) | copy-start | bytes 25165828
  29.7 5.4 %copy-start.1 = (f32[2,512,512,4]{2,1,3,0:T(8,128)}, f32[2,512,512,4]{2,1,3,0:T(8,128)S(1)}, u32[]{:S(2)}) copy-start(f32[2,512,512,4]{2,1,3,0:T(8,128)S(1)} %get-tuple-element.13) | copy-start | bytes 25165828
  40.4 54.0 %collective-permute-start.4 = (f32[512,256]{1,0:T(8,128)}, f32[512,256]{1,0:T(8,128)}, u32[]{:S(2)}, u32[]{:S(2)}) collective-permute-start(f32[512,256]{1,0:T(8,128)} %copy.82), channel_id=1, source_target_pairs={{4,0},{8,4},{12,8},{16,12},{20,16},{24,20},{28,24},{32,28},{36,32}... | collective-permute-start | bytes 1572872 | tf_op jit(solution)/shard_map/ppermute | solution.py:17
  71.4 7.8 %copy-start.2 = (bf16[2,4,512,512]{2,3,1,0:T(8,128)(2,1)}, bf16[2,4,512,512]{2,3,1,0:T(8,128)(2,1)S(1)}, u32[]{:S(2)}) copy-start(bf16[2,4,512,512]{2,3,1,0:T(8,128)(2,1)S(1)} %get-tuple-element.9) | copy-start | bytes 12582916
  71.4 3.7 %copy-start.3 = (bf16[2,4,512,512]{2,3,1,0:T(8,128)(2,1)S(1)}, bf16[2,4,512,512]{2,3,1,0:T(8,128)(2,1)}, u32[]{:S(2)}) copy-start(bf16[2,4,512,512]{2,3,1,0:T(8,128)(2,1)} %get-tuple-element.8) | copy-start | bytes 12582916
  71.4 7.8 %copy-start.6 = (f32[2,512,128,1]{1,2,3,0:T(8,128)S(1)}, f32[2,512,128,1]{1,2,3,0:T(8,128)}, u32[]{:S(2)}) copy-start(f32[2,512,128,1]{1,2,3,0:T(8,128)} %fusion.10) | copy-start | bytes 1572868
  81.0 13.4 %copy-start.4 = (f32[512,256]{1,0:T(8,128)S(1)}, f32[512,256]{1,0:T(8,128)}, u32[]{:S(2)}) copy-start(f32[512,256]{1,0:T(8,128)} %copy.83) | copy-start | bytes 1572868
  84.6 29.2 %all-to-all-start = ((bf16[4,128,1024]{2,1,0:T(8,128)(2,1)}), bf16[4,128,1024]{2,1,0:T(8,128)(2,1)S(1)}, u32[]{:S(2)}, u32[]{:S(2)}) async-start(bf16[4,128,1024]{2,1,0:T(8,128)(2,1)} %convert_element_type.32), calls=%async_computation | async-start | bytes 2097152 | tf_op jit(solution)/shard_map/all_to_all | solution.py:128
  88.1 20.2 %collective-permute-start.3 = (f32[512,256]{1,0:T(8,128)}, f32[512,256]{1,0:T(8,128)}, u32[]{:S(2)}, u32[]{:S(2)}) collective-permute-start(f32[512,256]{1,0:T(8,128)} %copy.76), channel_id=1, source_target_pairs={{4,0},{8,4},{12,8},{16,12},{20,16},{24,20},{28,24},{32,28},{36,32}... | collective-permute-start | bytes 1572872 | tf_op jit(solution)/shard_map/ppermute | solution.py:17
where the time goes:
time: 116 us
  matrix products  36.7 us (32%)
  other arithmetic  23.3 us (20%)
  starting transfers between devices  20.5 us (18%)
  local copies, waits for them, and re-layouts  18.6 us (16%)
  waiting for transfers between devices  15.8 us (14%)
    dot_general x2, matrix products, value_terms(): jnp.einsum('rhgd,khd->hgrk', gradient_pieces, value_pieces, preferred_ele...  17.5 us
    ppermute x5, starting transfers between devices, shifted(): return lax.ppermute(value, axis, pairs)  17 us
    convert_element_type x1, other arithmetic, block_gradients(): (probs_full * (grad_probs - delta_rows[..., None])).astype(jnp.bfloat16)  15.2 us
    ppermute x5, waiting for transfers between devices, shifted(): return lax.ppermute(value, axis, pairs)  12.1 us
    dot_general x2, matrix products, block_gradients(): jnp.einsum('hgrk,rhgd->khd', probs_round, gradient_pieces, preferred_elem...  6.51 us
    unnamed x19, local copies, waits for them, and re-layouts  6.16 us
    dot_general x2, matrix products, block_gradients(): jnp.einsum('hgrk,rhgd->khd', grad_scores, query_pieces, preferred_element...  5.95 us
    reduce_sum x2, other arithmetic, partial_stats(): jnp.sum(jnp.where(keep_mask, jnp.exp(scores - row_top[..., None]), 0.0),...  4.09 us
  transfers between devices with their start and end apart: 6, of which 2 were waited for; matrix products, arithmetic and copies ran while one was open for 64% of the time, Pallas kernels for 0%

commit v1 on v0

v1 whole, which is shorter than its diff:
```python
import functools
import math

import jax
import jax.numpy as jnp
from jax import lax
from jax.experimental import pallas as pl
from jax.experimental.pallas import tpu as pltpu
from jax.sharding import PartitionSpec as P

HEAD = 128
TILE = 128
GROUPS = 2
SHARE = 4
BLOCK = 512
TILES = BLOCK // TILE
SPAN = BLOCK + TILE
WIDE = SHARE * HEAD
MASKED = -1e30
SCALE = 1.0 / math.sqrt(HEAD)
SCALE_LOG2 = SCALE * math.log2(math.e)
MESH = pl.DeviceIdType.MESH

NT = (((1,), (1,)), ((), ()))
NN = (((1,), (0,)), ((), ()))


def dot(a, b, dims):
    return lax.dot_general(a, b, dims, preferred_element_type=jnp.float32)


def kernel(
    n_seq,
    q_hbm, k_hbm, v_hbm, o_hbm, doc_hbm,
    dq_ref, dk_ref, dv_ref,
    q_s, o_s, k_s, v_s, kt_s, doc_s, docp_s, kdoc_s, bias_s, prob_s,
    dv_acc, dk_acc, back_s, back_r, dq_s,
    load_sem, kv_send, kv_recv, doc_send, doc_recv, dq_send, dq_recv, dq_own, back_send, back_recv,
):
    s = lax.axis_index("seq")
    h = lax.axis_index("head")
    following = (lax.rem(s + 1, n_seq), h)
    previous = (lax.rem(s + n_seq - 1, n_seq), h)

    loads = []

    def load(src, dst):
        copy = pltpu.make_async_copy(src, dst, load_sem.at[len(loads)])
        copy.start()
        loads.append(copy)

    load(doc_hbm, doc_s)
    for g in range(GROUPS):
        load(k_hbm.at[:, pl.ds(g * HEAD, HEAD)], k_s.at[g, pl.ds(BLOCK, BLOCK)])
        load(v_hbm.at[:, pl.ds(g * HEAD, HEAD)], v_s.at[g, pl.ds(BLOCK, BLOCK)])
    for r in range(GROUPS * SHARE):
        load(q_hbm.at[:, pl.ds(r * HEAD, HEAD)], q_s.at[r])
        load(o_hbm.at[:, pl.ds(r * HEAD, HEAD)], o_s.at[r])

    barrier = pltpu.get_barrier_semaphore()
    for peer in [following, previous] + [(s, lax.rem(h + d, 4)) for d in (1, 2, 3)]:
        pl.semaphore_signal(barrier, inc=1, device_id=peer, device_id_type=MESH)
    for copy in loads[: 1 + 2 * GROUPS]:
        copy.wait()
    pl.semaphore_wait(barrier, 5)

    doc_copy = pltpu.make_async_remote_copy(
        src_ref=doc_s, dst_ref=docp_s, send_sem=doc_send, recv_sem=doc_recv,
        device_id=following, device_id_type=MESH,
    )
    doc_copy.start()

    def kv_copy(buffer, which, g, i):
        slot = (g * 2 + which) * TILES + i
        return pltpu.make_async_remote_copy(
            src_ref=buffer.at[g, pl.ds(pl.multiple_of(BLOCK + i * TILE, TILE), TILE)],
            dst_ref=buffer.at[g, pl.ds(pl.multiple_of(i * TILE, TILE), TILE)],
            send_sem=kv_send.at[slot], recv_sem=kv_recv.at[slot],
            device_id=following, device_id_type=MESH,
        )

    for g in range(GROUPS):
        for which, buffer in ((0, k_s), (1, v_s)):
            for i in reversed(range(TILES)):
                kv_copy(buffer, which, g, i).start()

    for g in range(GROUPS):
        for j in range(TILES):
            rows = pl.ds(BLOCK + j * TILE, TILE)
            kt_s[g, :, rows] = k_s[g, rows, :].T
    dv_acc[...] = jnp.zeros_like(dv_acc)
    dk_acc[...] = jnp.zeros_like(dk_acc)

    doc_copy.wait()
    doc_own = doc_s[...].astype(jnp.float32)
    doc_prev = jnp.where(s > 0, docp_s[...].astype(jnp.float32), -1.0)
    for j in range(2 * TILES):
        source = doc_prev if j < TILES else doc_own
        row = source[j % TILES : j % TILES + 1, :]
        kdoc_s[j] = jnp.broadcast_to(row, (TILE, TILE)).T
    key_at = lax.broadcasted_iota(jnp.int32, (TILE, TILE), 0)
    query_at = lax.broadcasted_iota(jnp.int32, (TILE, TILE), 1)
    for i in range(TILES):
        query_doc = doc_own[i : i + 1, :]
        for j in range(TILES + 1):
            keep = kdoc_s[i + j] == query_doc
            if j == 0:
                keep = keep & (key_at > query_at)
            if j == TILES:
                keep = keep & (key_at <= query_at)
            bias_s[i, pl.ds(j * TILE, TILE), :] = jnp.where(keep, 0.0, MASKED)
    for copy in loads[1 + 2 * GROUPS :]:
        copy.wait()

    def back_copy(slot):
        return pltpu.make_async_remote_copy(
            src_ref=back_s.at[slot], dst_ref=back_r.at[slot],
            send_sem=back_send.at[slot], recv_sem=back_recv.at[slot],
            device_id=previous, device_id_type=MESH,
        )

    def dq_columns(owner, g):
        return pl.ds(pl.multiple_of(owner * (GROUPS * WIDE) + g * WIDE, WIDE), WIDE)

    def dq_copy(g, i):
        return pltpu.make_async_remote_copy(
            src_ref=dq_s.at[g * TILES + i], dst_ref=dq_ref.at[:, dq_columns(h, g)],
            send_sem=dq_send.at[g * TILES + i], recv_sem=dq_recv.at[g * TILES + h],
            device_id=(s, i), device_id_type=MESH,
        )

    def dq_local(g):
        return pltpu.make_async_copy(
            dq_s.at[g * TILES + h], dq_ref.at[:, dq_columns(h, g)], dq_own.at[g]
        )

    for g in range(GROUPS):
        def forward(step, carry, g=g):
            i = TILES - 1 - step
            kv_copy(k_s, 0, g, i).wait()
            rows = pl.ds(pl.multiple_of(i * TILE, TILE), TILE)
            span = pl.ds(pl.multiple_of(i * TILE, TILE), SPAN)
            kt_s[g, :, rows] = k_s[g, rows, :].T
            keys = k_s[g, span, :]
            bias = bias_s[i]
            rounded, outs = [], []
            for r in range(SHARE):
                scores = dot(keys, q_s[g * SHARE + r, rows, :], NT) * SCALE_LOG2 + bias
                top = jnp.max(scores, axis=0, keepdims=True)
                grown = jnp.exp2(scores - top)
                probs = grown * (1.0 / jnp.sum(grown, axis=0, keepdims=True))
                prob_s[i, :, pl.ds(r * HEAD, HEAD)] = probs
                rounded.append(probs.astype(jnp.bfloat16))
                outs.append(o_s[g * SHARE + r, rows, :])
            dv_acc[g, span, :] += dot(
                jnp.concatenate(rounded, axis=1), jnp.concatenate(outs, axis=0), NN
            )
            return carry

        lax.fori_loop(0, TILES, forward, 0)
        back_s[2 * g] = dv_acc[g, pl.ds(0, BLOCK), :].astype(jnp.bfloat16)
        back_copy(2 * g).start()

        def backward(step, carry, g=g):
            i = TILES - 1 - step
            kv_copy(v_s, 1, g, i).wait()
            rows = pl.ds(pl.multiple_of(i * TILE, TILE), TILE)
            span = pl.ds(pl.multiple_of(i * TILE, TILE), SPAN)
            values = v_s[g, span, :]
            rounded, queries = [], []
            for r in range(SHARE):
                grad_probs = dot(values, o_s[g * SHARE + r, rows, :], NT)
                probs = prob_s[i, :, pl.ds(r * HEAD, HEAD)]
                delta = jnp.sum(probs * grad_probs, axis=0, keepdims=True)
                rounded.append((probs * (grad_probs - delta)).astype(jnp.bfloat16))
                queries.append(q_s[g * SHARE + r, rows, :])
            grad_scores = jnp.concatenate(rounded, axis=1)
            dk_acc[g, span, :] += dot(grad_scores, jnp.concatenate(queries, axis=0), NN)
            dq_t = dot(kt_s[g, :, span], grad_scores, NN) * SCALE
            slot = g * TILES + i
            for r in range(SHARE):
                dq_s[slot, :, pl.ds(r * HEAD, HEAD)] = (
                    dq_t[:, r * HEAD : (r + 1) * HEAD].T.astype(jnp.bfloat16)
                )

            @pl.when(i != h)
            def _():
                dq_copy(g, i).start()

            @pl.when(i == h)
            def _():
                dq_local(g).start()

            return carry

        lax.fori_loop(0, TILES, backward, 0)
        back_s[2 * g + 1] = (dk_acc[g, pl.ds(0, BLOCK), :] * SCALE).astype(jnp.bfloat16)
        back_copy(2 * g + 1).start()

    for g in range(GROUPS):
        columns = pl.ds(g * HEAD, HEAD)
        back_copy(2 * g).wait()
        dv_ref[:, columns] = (
            dv_acc[g, pl.ds(BLOCK, BLOCK), :] + back_r[2 * g].astype(jnp.float32)
        ).astype(jnp.bfloat16)
        back_copy(2 * g + 1).wait()
        dk_ref[:, columns] = (
            dk_acc[g, pl.ds(BLOCK, BLOCK), :] * SCALE + back_r[2 * g + 1].astype(jnp.float32)
        ).astype(jnp.bfloat16)

    for g in range(GROUPS):
        dq_local(g).wait()
        for i in range(TILES):
            @pl.when(i != h)
            def _(g=g, i=i):
                dq_copy(g, i).wait_send()

        for d in (1, 2, 3):
            owner = lax.rem(h + d, 4)
            pltpu.make_async_remote_copy(
                src_ref=dq_s.at[g * TILES], dst_ref=dq_ref.at[:, dq_columns(owner, g)],
                send_sem=dq_send.at[g * TILES], recv_sem=dq_recv.at[g * TILES + owner],
                device_id=(s, owner), device_id_type=MESH,
            ).wait_recv()


def local(n_seq, queries, key_heads, value_head_rows, out_grad, doc_ids):
    bf16, f32 = jnp.bfloat16, jnp.float32
    dma = pltpu.SemaphoreType.DMA
    anywhere = pl.BlockSpec(memory_space=pl.ANY)
    vmem = pl.BlockSpec(memory_space=pltpu.VMEM)
    return pl.pallas_call(
        functools.partial(kernel, n_seq),
        out_shape=(
            jax.ShapeDtypeStruct((TILE, 4 * GROUPS * WIDE), bf16),
            jax.ShapeDtypeStruct((BLOCK, GROUPS * HEAD), bf16),
            jax.ShapeDtypeStruct((BLOCK, GROUPS * HEAD), bf16),
        ),
        in_specs=[anywhere] * 5,
        out_specs=(vmem, vmem, vmem),
        scratch_shapes=[
            pltpu.VMEM((GROUPS * SHARE, BLOCK, HEAD), bf16),
            pltpu.VMEM((GROUPS * SHARE, BLOCK, HEAD), bf16),
            pltpu.VMEM((GROUPS, 2 * BLOCK, HEAD), bf16),
            pltpu.VMEM((GROUPS, 2 * BLOCK, HEAD), bf16),
            pltpu.VMEM((GROUPS, HEAD, 2 * BLOCK), bf16),
            pltpu.VMEM((TILES, TILE), jnp.int32),
            pltpu.VMEM((TILES, TILE), jnp.int32),
            pltpu.VMEM((2 * TILES, TILE, TILE), f32),
            pltpu.VMEM((TILES, SPAN, TILE), f32),
            pltpu.VMEM((TILES, SPAN, WIDE), f32),
            pltpu.VMEM((GROUPS, 2 * BLOCK, HEAD), f32),
            pltpu.VMEM((GROUPS, 2 * BLOCK, HEAD), f32),
            pltpu.VMEM((2 * GROUPS, BLOCK, HEAD), bf16),
            pltpu.VMEM((2 * GROUPS, BLOCK, HEAD), bf16),
            pltpu.VMEM((GROUPS * TILES, TILE, WIDE), bf16),
            dma((1 + 2 * GROUPS + 2 * GROUPS * SHARE,)),
            dma((2 * GROUPS * TILES,)),
            dma((2 * GROUPS * TILES,)),
            dma(()),
            dma(()),
            dma((GROUPS * TILES,)),
            dma((GROUPS * TILES,)),
            dma((GROUPS,)),
            dma((2 * GROUPS,)),
            dma((2 * GROUPS,)),
        ],
        compiler_params=pltpu.CompilerParams(
            collective_id=0, has_side_effects=True, vmem_limit_bytes=48 * 2**20
        ),
    )(*[pltpu.with_memory_space_constraint(a, pltpu.HBM) for a in (queries, key_heads, value_head_rows, out_grad, doc_ids.reshape(TILES, TILE))])


def solution(mesh):
    placed = (P("seq", "head"), P("seq", "head"), P("seq", "head"), P("seq", "head"), P("seq"))
    return jax.shard_map(
        functools.partial(local, mesh.shape["seq"]),
        mesh=mesh,
        in_specs=placed,
        out_specs=(P(("seq", "head"), None), P("seq", "head"), P("seq", "head")),
        check_vma=False,
    )
```

time: 116 us -> 39.1 us (0.34)
  matrix products: 36.7 us -> 0 us
  Pallas kernels: 0 us -> 36 us
  other arithmetic: 23.3 us -> 0 us
  starting transfers between devices: 20.5 us -> 0 us
  local copies, waits for them, and re-layouts: 18.6 us -> 2.38 us
  waiting for transfers between devices: 15.8 us -> 0 us
    dot_general x10 -> x0, matrix products: 36.7 us -> none  [the longest x2 17.5 us: value_terms(): jnp.einsum('rhgd,khd->hgrk', gradient_pieces, value_pieces, preferred_ele...]
    pallas_call x0 -> x1, Pallas kernels: none -> 36 us  [local(): pl.pallas_call(functools.partial(kernel, n_seq), out_shape=(jax.ShapeDtyp...]
    convert_element_type x3 -> x0, other arithmetic: 18.8 us -> none  [the longest x1 15.2 us: block_gradients(): (probs_full * (grad_probs - delta_rows[..., None])).astype(jnp.bfloat16)]
    ppermute x5 -> x0, starting transfers between devices: 17 us -> none  [shifted(): return lax.ppermute(value, axis, pairs)]
    ppermute x5 -> x0, waiting for transfers between devices: 12.1 us -> none  [shifted(): return lax.ppermute(value, axis, pairs)]
    reshape x8 -> x0, local copies, waits for them, and re-layouts: 9.38 us -> none  [the longest x2 3.07 us: block_gradients(): value_portion.reshape(key_number, -1)]
    reduce_sum x2 -> x0, other arithmetic: 4.09 us -> none  [partial_stats(): jnp.sum(jnp.where(keep_mask, jnp.exp(scores - row_top[..., None]), 0.0),...]
    unnamed x19 -> x3, local copies, waits for them, and re-layouts: 6.16 us -> 2.38 us
  transfers between devices with their start and end apart: 6 -> 0, of which waited for: 2 -> 0; matrix products, arithmetic and copies ran while one was open for 64% -> 0% of each run, Pallas kernels for 0% -> 0%
where the time goes in v1:
time: 39.1 us; the launch traced here: 39 us
  Pallas kernels  36 us (92%)
  local copies, waits for them, and re-layouts  2.38 us (6%)
  between operations  0.64 us (2%)
    pallas_call x1, Pallas kernels, local(): pl.pallas_call(functools.partial(kernel, n_seq), out_shape=(jax.ShapeDtyp...  36 us
    unnamed x3, local copies, waits for them, and re-layouts  2.38 us

profile of v1, /device:TPU:102, one launch (start us, length us, event | category | flops | bytes accessed | tf_op | source)
XLA Modules:
  0.0 39.0 jit_solution(2223041545478424050)
XLA Ops:
  0.6 36.0 %shard_map.76 = (bf16[128,4096]{1,0:T(8,128)(2,1)S(1)}, bf16[512,256]{1,0:T(8,128)(2,1)S(1)}, bf16[512,256]{1,0:T(8,128)(2,1)S(1)}) custom-call(bf16[512,1024]{1,0:T(8,128)(2,1)} %q_hbm.1, bf16[512,256]{1,0:T(8,128)(2,1)} %k_hbm.1, bf16[512,256]{1,0:T(8,128)(2,1)} %v_hbm.1, bf16[512,1024]{1,0:T(8,128)(2,1)} %o_hbm.1, s32[4,128]{1,0:T(4,128)} %bitcast.1), custom_call_target="tpu_custom_call" | custom-call | tf_op jit(solution)/shard_map/pallas_call | solution.py:232
  36.6 1.0 %copy.11 = bf16[128,4096]{1,0:T(8,128)(2,1)} copy(bf16[128,4096]{1,0:T(8,128)(2,1)S(1)} %get-tuple-element.6) | data formatting | bytes 2097152
  37.6 0.7 %copy.12 = bf16[512,256]{1,0:T(8,128)(2,1)} copy(bf16[512,256]{1,0:T(8,128)(2,1)S(1)} %get-tuple-element.7) | data formatting | bytes 524288
  38.3 0.7 %copy.13 = bf16[512,256]{1,0:T(8,128)(2,1)} copy(bf16[512,256]{1,0:T(8,128)(2,1)S(1)} %get-tuple-element.8) | data formatting | bytes 524288

commit v2 on v1

--- a/solution.py
+++ b/solution.py
@@ -16,6 +16,7 @@
 TILES = BLOCK // TILE
 SPAN = BLOCK + TILE
 WIDE = SHARE * HEAD
+PAIR = 2
 MASKED = -1e30
 SCALE = 1.0 / math.sqrt(HEAD)
 SCALE_LOG2 = SCALE * math.log2(math.e)
@@ -23,6 +24,7 @@
 
 NT = (((1,), (1,)), ((), ()))
 NN = (((1,), (0,)), ((), ()))
+TN = (((0,), (0,)), ((), ()))
 
 
 def dot(a, b, dims):
@@ -33,7 +35,7 @@
     n_seq,
     q_hbm, k_hbm, v_hbm, o_hbm, doc_hbm,
     dq_ref, dk_ref, dv_ref,
-    q_s, o_s, k_s, v_s, kt_s, doc_s, docp_s, kdoc_s, bias_s, prob_s,
+    q_s, o_s, k_s, v_s, doc_s, docp_s, kdoc_s, bias_s, prob_s,
     dv_acc, dk_acc, back_s, back_r, dq_s,
     load_sem, kv_send, kv_recv, doc_send, doc_recv, dq_send, dq_recv, dq_own, back_send, back_recv,
 ):
@@ -84,10 +86,6 @@
             for i in reversed(range(TILES)):
                 kv_copy(buffer, which, g, i).start()
 
-    for g in range(GROUPS):
-        for j in range(TILES):
-            rows = pl.ds(BLOCK + j * TILE, TILE)
-            kt_s[g, :, rows] = k_s[g, rows, :].T
     dv_acc[...] = jnp.zeros_like(dv_acc)
     dk_acc[...] = jnp.zeros_like(dk_acc)
 
@@ -140,18 +138,20 @@
             kv_copy(k_s, 0, g, i).wait()
             rows = pl.ds(pl.multiple_of(i * TILE, TILE), TILE)
             span = pl.ds(pl.multiple_of(i * TILE, TILE), SPAN)
-            kt_s[g, :, rows] = k_s[g, rows, :].T
             keys = k_s[g, span, :]
             bias = bias_s[i]
-            rounded, outs = [], []
-            for r in range(SHARE):
-                scores = dot(keys, q_s[g * SHARE + r, rows, :], NT) * SCALE_LOG2 + bias
-                top = jnp.max(scores, axis=0, keepdims=True)
-                grown = jnp.exp2(scores - top)
-                probs = grown * (1.0 / jnp.sum(grown, axis=0, keepdims=True))
-                prob_s[i, :, pl.ds(r * HEAD, HEAD)] = probs
-                rounded.append(probs.astype(jnp.bfloat16))
-                outs.append(o_s[g * SHARE + r, rows, :])
+            outs = [o_s[g * SHARE + r, rows, :] for r in range(SHARE)]
+            rounded = []
+            for r in range(0, SHARE, PAIR):
+                queries = [q_s[g * SHARE + e, rows, :] for e in range(r, r + PAIR)]
+                joined = dot(keys, jnp.concatenate(queries, axis=0), NT)
+                for e in range(PAIR):
+                    scores = joined[:, e * HEAD : (e + 1) * HEAD] * SCALE_LOG2 + bias
+                    top = jnp.max(scores, axis=0, keepdims=True)
+                    grown = jnp.exp2(scores - top)
+                    probs = grown * (1.0 / jnp.sum(grown, axis=0, keepdims=True))
+                    prob_s[i, :, pl.ds((r + e) * HEAD, HEAD)] = probs
+                    rounded.append(probs.astype(jnp.bfloat16))
             dv_acc[g, span, :] += dot(
                 jnp.concatenate(rounded, axis=1), jnp.concatenate(outs, axis=0), NN
             )
@@ -167,20 +167,23 @@
             rows = pl.ds(pl.multiple_of(i * TILE, TILE), TILE)
             span = pl.ds(pl.multiple_of(i * TILE, TILE), SPAN)
             values = v_s[g, span, :]
-            rounded, queries = [], []
-            for r in range(SHARE):
-                grad_probs = dot(values, o_s[g * SHARE + r, rows, :], NT)
-                probs = prob_s[i, :, pl.ds(r * HEAD, HEAD)]
-                delta = jnp.sum(probs * grad_probs, axis=0, keepdims=True)
-                rounded.append((probs * (grad_probs - delta)).astype(jnp.bfloat16))
-                queries.append(q_s[g * SHARE + r, rows, :])
+            queries = [q_s[g * SHARE + r, rows, :] for r in range(SHARE)]
+            rounded = []
+            for r in range(0, SHARE, PAIR):
+                outs = [o_s[g * SHARE + e, rows, :] for e in range(r, r + PAIR)]
+                joined = dot(values, jnp.concatenate(outs, axis=0), NT)
+                for e in range(PAIR):
+                    grad_probs = joined[:, e * HEAD : (e + 1) * HEAD]
+                    probs = prob_s[i, :, pl.ds((r + e) * HEAD, HEAD)]
+                    delta = jnp.sum(probs * grad_probs, axis=0, keepdims=True)
+                    rounded.append((probs * (grad_probs - delta)).astype(jnp.bfloat16))
             grad_scores = jnp.concatenate(rounded, axis=1)
             dk_acc[g, span, :] += dot(grad_scores, jnp.concatenate(queries, axis=0), NN)
-            dq_t = dot(kt_s[g, :, span], grad_scores, NN) * SCALE
             slot = g * TILES + i
+            grads = dot(grad_scores, k_s[g, span, :], TN) * SCALE
             for r in range(SHARE):
                 dq_s[slot, :, pl.ds(r * HEAD, HEAD)] = (
-                    dq_t[:, r * HEAD : (r + 1) * HEAD].T.astype(jnp.bfloat16)
+                    grads[r * HEAD : (r + 1) * HEAD, :].astype(jnp.bfloat16)
                 )
 
             @pl.when(i != h)
@@ -224,18 +227,30 @@
             ).wait_recv()
 
 
+def write_out(a_ref, b_ref, c_ref, a_out, b_out, c_out, sem):
+    copies = [
+        pltpu.make_async_copy(src, dst, sem.at[slot])
+        for slot, (src, dst) in enumerate(((a_ref, a_out), (b_ref, b_out), (c_ref, c_out)))
+    ]
+    for copy in copies:
+        copy.start()
+    for copy in copies:
+        copy.wait()
+
+
 def local(n_seq, queries, key_heads, value_head_rows, out_grad, doc_ids):
     bf16, f32 = jnp.bfloat16, jnp.float32
     dma = pltpu.SemaphoreType.DMA
     anywhere = pl.BlockSpec(memory_space=pl.ANY)
     vmem = pl.BlockSpec(memory_space=pltpu.VMEM)
-    return pl.pallas_call(
-        functools.partial(kernel, n_seq),
-        out_shape=(
+    shapes = (
             jax.ShapeDtypeStruct((TILE, 4 * GROUPS * WIDE), bf16),
             jax.ShapeDtypeStruct((BLOCK, GROUPS * HEAD), bf16),
             jax.ShapeDtypeStruct((BLOCK, GROUPS * HEAD), bf16),
-        ),
+    )
+    grads = pl.pallas_call(
+        functools.partial(kernel, n_seq),
+        out_shape=shapes,
         in_specs=[anywhere] * 5,
         out_specs=(vmem, vmem, vmem),
         scratch_shapes=[
@@ -243,7 +258,6 @@
             pltpu.VMEM((GROUPS * SHARE, BLOCK, HEAD), bf16),
             pltpu.VMEM((GROUPS, 2 * BLOCK, HEAD), bf16),
             pltpu.VMEM((GROUPS, 2 * BLOCK, HEAD), bf16),
-            pltpu.VMEM((GROUPS, HEAD, 2 * BLOCK), bf16),
             pltpu.VMEM((TILES, TILE), jnp.int32),
             pltpu.VMEM((TILES, TILE), jnp.int32),
             pltpu.VMEM((2 * TILES, TILE, TILE), f32),
@@ -270,6 +284,14 @@
         ),
     )(*[pltpu.with_memory_space_constraint(a, pltpu.HBM) for a in (queries, key_heads, value_head_rows, out_grad, doc_ids.reshape(TILES, TILE))])
 
+    return pl.pallas_call(
+        write_out,
+        out_shape=shapes,
+        in_specs=[vmem] * 3,
+        out_specs=(anywhere,) * 3,
+        scratch_shapes=[dma((3,))],
+    )(*[pltpu.with_memory_space_constraint(a, pltpu.VMEM) for a in grads])
+
 
 def solution(mesh):
     placed = (P("seq", "head"), P("seq", "head"), P("seq", "head"), P("seq", "head"), P("seq"))

time: 39.1 us -> 37.9 us (0.969)
  local copies, waits for them, and re-layouts: 2.38 us -> 0 us
  Pallas kernels: 36 us -> 37.1 us
    unnamed x3 -> x0, local copies, waits for them, and re-layouts: 2.38 us -> none
    pallas_call x1 -> x2, Pallas kernels: 36 us -> 37.1 us  [the longest x1 36 us: local(): pl.pallas_call(functools.partial(kernel, n_seq), out_shape=shapes, in_spe...]
where the time goes in v2:
time: 37.9 us; the launch traced here: 37.8 us
  Pallas kernels  37.1 us (98%)
  between operations  0.64 us (2%)
    pallas_call x1, Pallas kernels, local(): pl.pallas_call(functools.partial(kernel, n_seq), out_shape=shapes, in_spe...  36 us
    pallas_call x1, Pallas kernels, local(): pl.pallas_call(write_out, out_shape=shapes, in_specs=[vmem] * 3, out_spec...  1.16 us

profile of v2, /device:TPU:102, one launch (start us, length us, event | category | flops | bytes accessed | tf_op | source)
XLA Modules:
  0.0 37.8 jit_solution(5097273246965811736)
XLA Ops:
  0.6 36.0 %shard_map.76 = (bf16[128,4096]{1,0:T(8,128)(2,1)S(1)}, bf16[512,256]{1,0:T(8,128)(2,1)S(1)}, bf16[512,256]{1,0:T(8,128)(2,1)S(1)}) custom-call(bf16[512,1024]{1,0:T(8,128)(2,1)} %q_hbm.1, bf16[512,256]{1,0:T(8,128)(2,1)} %k_hbm.1, bf16[512,256]{1,0:T(8,128)(2,1)} %v_hbm.1, bf16[512,1024]{1,0:T(8,128)(2,1)} %o_hbm.1, s32[4,128]{1,0:T(4,128)} %bitcast.1), custom_call_target="tpu_custom_call" | custom-call | tf_op jit(solution)/shard_map/pallas_call | solution.py:251
  36.6 1.2 %shard_map.77 = (bf16[128,4096]{1,0:T(8,128)(2,1)}, bf16[512,256]{1,0:T(8,128)(2,1)}, bf16[512,256]{1,0:T(8,128)(2,1)}) custom-call(bf16[128,4096]{1,0:T(8,128)(2,1)S(1)} %get-tuple-element.6.a_ref, bf16[512,256]{1,0:T(8,128)(2,1)S(1)} %get-tuple-element.7.b_ref, bf16[512,256]{1,0:T(8,128)(2,1)S(1)} %get-tuple-element.8.c_ref), custom_call_target="tpu_custom_call" | custom-call | tf_op jit(solution)/shard_map/pallas_call | solution.py:287

commit v3 on v2

--- a/solution.py
+++ b/solution.py
@@ -17,6 +17,9 @@
 SPAN = BLOCK + TILE
 WIDE = SHARE * HEAD
 PAIR = 2
+LINE = 4
+RELAYED = (2,)
+PARTS = ((3, 2), (1, 0))
 MASKED = -1e30
 SCALE = 1.0 / math.sqrt(HEAD)
 SCALE_LOG2 = SCALE * math.log2(math.e)
@@ -35,14 +38,18 @@
     n_seq,
     q_hbm, k_hbm, v_hbm, o_hbm, doc_hbm,
     dq_ref, dk_ref, dv_ref,
-    q_s, o_s, k_s, v_s, doc_s, docp_s, kdoc_s, bias_s, prob_s,
-    dv_acc, dk_acc, back_s, back_r, dq_s,
+    q_s, o_s, k_s, v_s, doc_s, docp_s, kdoc_s, bias_s, prob_s, share_s, outs_s,
+    dv_acc, dk_acc, back_s, back_r, relay_s, dq_s,
     load_sem, kv_send, kv_recv, doc_send, doc_recv, dq_send, dq_recv, dq_own, back_send, back_recv,
+    relay_send, relay_recv,
 ):
     s = lax.axis_index("seq")
     h = lax.axis_index("head")
     following = (lax.rem(s + 1, n_seq), h)
     previous = (lax.rem(s + n_seq - 1, n_seq), h)
+    place = lax.rem(s, LINE)
+    first, third = place == 0, place == 2
+    partner = (lax.rem(s + jnp.where(place < 2, n_seq - 2, 2), n_seq), h)
 
     loads = []
 
@@ -60,11 +67,11 @@
         load(o_hbm.at[:, pl.ds(r * HEAD, HEAD)], o_s.at[r])
 
     barrier = pltpu.get_barrier_semaphore()
-    for peer in [following, previous] + [(s, lax.rem(h + d, 4)) for d in (1, 2, 3)]:
+    for peer in [following, previous, partner] + [(s, lax.rem(h + d, 4)) for d in (1, 2, 3)]:
         pl.semaphore_signal(barrier, inc=1, device_id=peer, device_id_type=MESH)
     for copy in loads[: 1 + 2 * GROUPS]:
         copy.wait()
-    pl.semaphore_wait(barrier, 5)
+    pl.semaphore_wait(barrier, 6)
 
     doc_copy = pltpu.make_async_remote_copy(
         src_ref=doc_s, dst_ref=docp_s, send_sem=doc_send, recv_sem=doc_recv,
@@ -117,6 +124,41 @@
             device_id=previous, device_id_type=MESH,
         )
 
+    def relay_copy(slot):
+        lane = RELAYED.index(slot)
+        return pltpu.make_async_remote_copy(
+            src_ref=back_s.at[slot], dst_ref=relay_s.at[lane],
+            send_sem=back_send.at[slot], recv_sem=relay_recv.at[lane],
+            device_id=partner, device_id_type=MESH,
+        )
+
+    def onward_copy(slot):
+        lane = RELAYED.index(slot)
+        return pltpu.make_async_remote_copy(
+            src_ref=relay_s.at[lane], dst_ref=back_r.at[slot],
+            send_sem=relay_send.at[lane], recv_sem=back_recv.at[slot],
+            device_id=following, device_id_type=MESH,
+        )
+
+    def send_back(slot):
+        if slot not in RELAYED:
+            back_copy(slot).start()
+            return
+
+        @pl.when(first)
+        def _():
+            relay_copy(slot).start()
+
+        @pl.when(jnp.logical_not(first))
+        def _():
+            back_copy(slot).start()
+
+    def pass_on(slot):
+        @pl.when(third)
+        def _():
+            relay_copy(slot).wait_recv()
+            onward_copy(slot).start()
+
     def dq_columns(owner, g):
         return pl.ds(pl.multiple_of(owner * (GROUPS * WIDE) + g * WIDE, WIDE), WIDE)
 
@@ -132,73 +174,84 @@
             dq_s.at[g * TILES + h], dq_ref.at[:, dq_columns(h, g)], dq_own.at[g]
         )
 
-    for g in range(GROUPS):
-        def forward(step, carry, g=g):
-            i = TILES - 1 - step
-            kv_copy(k_s, 0, g, i).wait()
-            rows = pl.ds(pl.multiple_of(i * TILE, TILE), TILE)
-            span = pl.ds(pl.multiple_of(i * TILE, TILE), SPAN)
-            keys = k_s[g, span, :]
-            bias = bias_s[i]
-            outs = [o_s[g * SHARE + r, rows, :] for r in range(SHARE)]
-            rounded = []
-            for r in range(0, SHARE, PAIR):
-                queries = [q_s[g * SHARE + e, rows, :] for e in range(r, r + PAIR)]
-                joined = dot(keys, jnp.concatenate(queries, axis=0), NT)
-                for e in range(PAIR):
-                    scores = joined[:, e * HEAD : (e + 1) * HEAD] * SCALE_LOG2 + bias
-                    top = jnp.max(scores, axis=0, keepdims=True)
-                    grown = jnp.exp2(scores - top)
-                    probs = grown * (1.0 / jnp.sum(grown, axis=0, keepdims=True))
-                    prob_s[i, :, pl.ds((r + e) * HEAD, HEAD)] = probs
-                    rounded.append(probs.astype(jnp.bfloat16))
-            dv_acc[g, span, :] += dot(
-                jnp.concatenate(rounded, axis=1), jnp.concatenate(outs, axis=0), NN
+    def forward(g, i):
+        rows, span = pl.ds(i * TILE, TILE), pl.ds(i * TILE, SPAN)
+        keys = k_s[g, span, :]
+        bias = bias_s[i]
+        for r in range(0, SHARE, PAIR):
+            queries = [q_s[g * SHARE + e, rows, :] for e in range(r, r + PAIR)]
+            joined = dot(keys, jnp.concatenate(queries, axis=0), NT)
+            for e in range(PAIR):
+                scores = joined[:, e * HEAD : (e + 1) * HEAD] * SCALE_LOG2 + bias
+                top = jnp.max(scores, axis=0, keepdims=True)
+                grown = jnp.exp2(scores - top)
+                share = 1.0 / jnp.sum(grown, axis=0, keepdims=True)
+                prob_s[i, :, pl.ds((r + e) * HEAD, HEAD)] = grown.astype(jnp.bfloat16)
+                share_s[i, pl.ds(r + e, 1), :] = share
+                column = jnp.broadcast_to(share, (TILE, TILE)).T
+                outs = o_s[g * SHARE + r + e, rows, :].astype(jnp.float32) * column
+                outs_s[i, pl.ds((r + e) * TILE, TILE), :] = outs.astype(jnp.bfloat16)
+        dv_acc[g, span, :] += dot(prob_s[i], outs_s[i], NN)
+
+    def backward(g, i):
+        rows, span = pl.ds(i * TILE, TILE), pl.ds(i * TILE, SPAN)
+        values = v_s[g, span, :]
+        queries = [q_s[g * SHARE + r, rows, :] for r in range(SHARE)]
+        rounded = []
+        for r in range(0, SHARE, PAIR):
+            joined = dot(values, outs_s[i, pl.ds(r * TILE, PAIR * TILE), :], NT)
+            for e in range(PAIR):
+                grad_probs = joined[:, e * HEAD : (e + 1) * HEAD]
+                grown = prob_s[i, :, pl.ds((r + e) * HEAD, HEAD)].astype(jnp.float32)
+                delta = jnp.sum(grown * grad_probs, axis=0, keepdims=True)
+                delta = delta * share_s[i, pl.ds(r + e, 1), :]
+                rounded.append((grown * (grad_probs - delta)).astype(jnp.bfloat16))
+        grad_scores = jnp.concatenate(rounded, axis=1)
+        dk_acc[g, span, :] += dot(grad_scores, jnp.concatenate(queries, axis=0), NN)
+        slot = g * TILES + i
+        grads = dot(grad_scores, k_s[g, span, :], TN) * SCALE
+        for r in range(SHARE):
+            dq_s[slot, :, pl.ds(r * HEAD, HEAD)] = (
+                grads[r * HEAD : (r + 1) * HEAD, :].astype(jnp.bfloat16)
             )
-            return carry
-
-        lax.fori_loop(0, TILES, forward, 0)
+
+
+    def dq_start(g, i):
+        @pl.when(i != h)
+        def _():
+            dq_copy(g, i).start()
+
+        @pl.when(i == h)
+        def _():
+            dq_local(g).start()
+
+    def forward_phase(g, parts):
+        for part in parts:
+            for i in part:
+                kv_copy(k_s, 0, g, i).wait()
+            for i in part:
+                forward(g, i)
         back_s[2 * g] = dv_acc[g, pl.ds(0, BLOCK), :].astype(jnp.bfloat16)
-        back_copy(2 * g).start()
-
-        def backward(step, carry, g=g):
-            i = TILES - 1 - step
-            kv_copy(v_s, 1, g, i).wait()
-            rows = pl.ds(pl.multiple_of(i * TILE, TILE), TILE)
-            span = pl.ds(pl.multiple_of(i * TILE, TILE), SPAN)
-            values = v_s[g, span, :]
-            queries = [q_s[g * SHARE + r, rows, :] for r in range(SHARE)]
-            rounded = []
-            for r in range(0, SHARE, PAIR):
-                outs = [o_s[g * SHARE + e, rows, :] for e in range(r, r + PAIR)]
-                joined = dot(values, jnp.concatenate(outs, axis=0), NT)
-                for e in range(PAIR):
-                    grad_probs = joined[:, e * HEAD : (e + 1) * HEAD]
-                    probs = prob_s[i, :, pl.ds((r + e) * HEAD, HEAD)]
-                    delta = jnp.sum(probs * grad_probs, axis=0, keepdims=True)
-                    rounded.append((probs * (grad_probs - delta)).astype(jnp.bfloat16))
-            grad_scores = jnp.concatenate(rounded, axis=1)
-            dk_acc[g, span, :] += dot(grad_scores, jnp.concatenate(queries, axis=0), NN)
-            slot = g * TILES + i
-            grads = dot(grad_scores, k_s[g, span, :], TN) * SCALE
-            for r in range(SHARE):
-                dq_s[slot, :, pl.ds(r * HEAD, HEAD)] = (
-                    grads[r * HEAD : (r + 1) * HEAD, :].astype(jnp.bfloat16)
-                )
-
-            @pl.when(i != h)
-            def _():
-                dq_copy(g, i).start()
-
-            @pl.when(i == h)
-            def _():
-                dq_local(g).start()
-
-            return carry
-
-        lax.fori_loop(0, TILES, backward, 0)
-        back_s[2 * g + 1] = (dk_acc[g, pl.ds(0, BLOCK), :] * SCALE).astype(jnp.bfloat16)
-        back_copy(2 * g + 1).start()
+        send_back(2 * g)
+
+    def backward_phase(g, parts):
+        for part in parts:
+            for i in part:
+                kv_copy(v_s, 1, g, i).wait()
+            for i in part:
+                backward(g, i)
+            if part is parts[-1]:
+                back_s[2 * g + 1] = (dk_acc[g, pl.ds(0, BLOCK), :] * SCALE).astype(jnp.bfloat16)
+                send_back(2 * g + 1)
+            for i in part:
+                dq_start(g, i)
+
+    for g in range(GROUPS):
+        forward_phase(g, PARTS)
+        backward_phase(g, PARTS)
+
+    for slot in RELAYED:
+        pass_on(slot)
 
     for g in range(GROUPS):
         columns = pl.ds(g * HEAD, HEAD)
@@ -210,6 +263,11 @@
         dk_ref[:, columns] = (
             dk_acc[g, pl.ds(BLOCK, BLOCK), :] * SCALE + back_r[2 * g + 1].astype(jnp.float32)
         ).astype(jnp.bfloat16)
+
+    for slot in RELAYED:
+        @pl.when(third)
+        def _(slot=slot):
+            onward_copy(slot).wait_send()
 
     for g in range(GROUPS):
         dq_local(g).wait()
@@ -262,11 +320,14 @@
             pltpu.VMEM((TILES, TILE), jnp.int32),
             pltpu.VMEM((2 * TILES, TILE, TILE), f32),
             pltpu.VMEM((TILES, SPAN, TILE), f32),
-            pltpu.VMEM((TILES, SPAN, WIDE), f32),
+            pltpu.VMEM((TILES, SPAN, WIDE), bf16),
+            pltpu.VMEM((TILES, 8, TILE), f32),
+            pltpu.VMEM((TILES, SHARE * TILE, HEAD), bf16),
             pltpu.VMEM((GROUPS, 2 * BLOCK, HEAD), f32),
             pltpu.VMEM((GROUPS, 2 * BLOCK, HEAD), f32),
             pltpu.VMEM((2 * GROUPS, BLOCK, HEAD), bf16),
             pltpu.VMEM((2 * GROUPS, BLOCK, HEAD), bf16),
+            pltpu.VMEM((len(RELAYED), BLOCK, HEAD), bf16),
             pltpu.VMEM((GROUPS * TILES, TILE, WIDE), bf16),
             dma((1 + 2 * GROUPS + 2 * GROUPS * SHARE,)),
             dma((2 * GROUPS * TILES,)),
@@ -278,6 +339,8 @@
             dma((GROUPS,)),
             dma((2 * GROUPS,)),
             dma((2 * GROUPS,)),
+            dma((len(RELAYED),)),
+            dma((len(RELAYED),)),
         ],
         compiler_params=pltpu.CompilerParams(
             collective_id=0, has_side_effects=True, vmem_limit_bytes=48 * 2**20

time: 37.9 us -> 36.5 us (0.963)
  the two profiles are of different devices: /device:TPU:102 before, /device:TPU:4 now
where the time goes in v3:
time: 36.5 us; the launch traced here: 36.3 us
  Pallas kernels  35.7 us (98%)
  between operations  0.64 us (2%)
    pallas_call x1, Pallas kernels, local(): pl.pallas_call(functools.partial(kernel, n_seq), out_shape=shapes, in_spe...  34.5 us
    pallas_call x1, Pallas kernels, local(): pl.pallas_call(write_out, out_shape=shapes, in_specs=[vmem] * 3, out_spec...  1.16 us

profile of v3, /device:TPU:4, one launch (start us, length us, event | category | flops | bytes accessed | tf_op | source)
XLA Modules:
  0.0 36.3 jit_solution(1884472067809081366)
XLA Ops:
  0.6 34.5 %shard_map.76 = (bf16[128,4096]{1,0:T(8,128)(2,1)S(1)}, bf16[512,256]{1,0:T(8,128)(2,1)S(1)}, bf16[512,256]{1,0:T(8,128)(2,1)S(1)}) custom-call(bf16[512,1024]{1,0:T(8,128)(2,1)} %q_hbm.1, bf16[512,256]{1,0:T(8,128)(2,1)} %k_hbm.1, bf16[512,256]{1,0:T(8,128)(2,1)} %v_hbm.1, bf16[512,1024]{1,0:T(8,128)(2,1)} %o_hbm.1, s32[4,128]{1,0:T(4,128)} %bitcast.1), custom_call_target="tpu_custom_call" | custom-call | tf_op jit(solution)/shard_map/pallas_call | solution.py:309
  35.2 1.2 %shard_map.77 = (bf16[128,4096]{1,0:T(8,128)(2,1)}, bf16[512,256]{1,0:T(8,128)(2,1)}, bf16[512,256]{1,0:T(8,128)(2,1)}) custom-call(bf16[128,4096]{1,0:T(8,128)(2,1)S(1)} %get-tuple-element.6.a_ref, bf16[512,256]{1,0:T(8,128)(2,1)S(1)} %get-tuple-element.7.b_ref, bf16[512,256]{1,0:T(8,128)(2,1)S(1)} %get-tuple-element.8.c_ref), custom_call_target="tpu_custom_call" | custom-call | tf_op jit(solution)/shard_map/pallas_call | solution.py:350

commit v4 on v3

--- a/solution.py
+++ b/solution.py
@@ -16,7 +16,7 @@
 TILES = BLOCK // TILE
 SPAN = BLOCK + TILE
 WIDE = SHARE * HEAD
-PAIR = 2
+PAIR = 1
 LINE = 4
 RELAYED = (2,)
 PARTS = ((3, 2), (1, 0))
@@ -240,11 +240,11 @@
                 kv_copy(v_s, 1, g, i).wait()
             for i in part:
                 backward(g, i)
+            for i in part:
+                dq_start(g, i)
             if part is parts[-1]:
                 back_s[2 * g + 1] = (dk_acc[g, pl.ds(0, BLOCK), :] * SCALE).astype(jnp.bfloat16)
                 send_back(2 * g + 1)
-            for i in part:
-                dq_start(g, i)
 
     for g in range(GROUPS):
         forward_phase(g, PARTS)

time: 36.5 us -> 36.4 us (level)
  no operation moved by 1% of the time
where the time goes in v4:
time: 36.4 us; the launch traced here: 36.3 us
  Pallas kernels  35.7 us (98%)
  between operations  0.64 us (2%)
    pallas_call x1, Pallas kernels, local(): pl.pallas_call(functools.partial(kernel, n_seq), out_shape=shapes, in_spe...  34.5 us
    pallas_call x1, Pallas kernels, local(): pl.pallas_call(write_out, out_shape=shapes, in_specs=[vmem] * 3, out_spec...  1.16 us

profile of v4, /device:TPU:4, one launch (start us, length us, event | category | flops | bytes accessed | tf_op | source)
XLA Modules:
  0.0 36.3 jit_solution(15970825125921442505)
XLA Ops:
  0.6 34.5 %shard_map.76 = (bf16[128,4096]{1,0:T(8,128)(2,1)S(1)}, bf16[512,256]{1,0:T(8,128)(2,1)S(1)}, bf16[512,256]{1,0:T(8,128)(2,1)S(1)}) custom-call(bf16[512,1024]{1,0:T(8,128)(2,1)} %q_hbm.1, bf16[512,256]{1,0:T(8,128)(2,1)} %k_hbm.1, bf16[512,256]{1,0:T(8,128)(2,1)} %v_hbm.1, bf16[512,1024]{1,0:T(8,128)(2,1)} %o_hbm.1, s32[4,128]{1,0:T(4,128)} %bitcast.1), custom_call_target="tpu_custom_call" | custom-call | tf_op jit(solution)/shard_map/pallas_call | solution.py:309
  35.2 1.2 %shard_map.77 = (bf16[128,4096]{1,0:T(8,128)(2,1)}, bf16[512,256]{1,0:T(8,128)(2,1)}, bf16[512,256]{1,0:T(8,128)(2,1)}) custom-call(bf16[128,4096]{1,0:T(8,128)(2,1)S(1)} %get-tuple-element.6.a_ref, bf16[512,256]{1,0:T(8,128)(2,1)S(1)} %get-tuple-element.7.b_ref, bf16[512,256]{1,0:T(8,128)(2,1)S(1)} %get-tuple-element.8.c_ref), custom_call_target="tpu_custom_call" | custom-call | tf_op jit(solution)/shard_map/pallas_call | solution.py:350
